TPU v7x, 128 devices: a whole 4x4x4 slice. The times are simulated.
128 devices in a mesh: dp: 8 (over z, core), rank: 16 (over x, y).
Axes of the slice: x: 4, y: 4, z: 4, core: 2. Of those that a mesh axis runs over, the one named last changes fastest.
Arguments:
- acts: bfloat16 [384, 256, 4096], P('dp', None, 'rank'), may hold values from -6 to 6
- grads: bfloat16 [384, 256, 11008], P('dp', None, 'rank'), may hold values from -6 to 6
- proj_in: bfloat16 [4096, 64], P('rank'), may hold values from -0.09375 to 0.09375
- proj_out: bfloat16 [11008, 64], P('rank'), may hold values from -0.0546875 to 0.0546875
- queries: float32 [4096, 4096], P('rank'), may hold values from -0.09375 to 0.09375
- seg_emb: int32 [384], P('dp'), may hold values from 0 to 15
- query_emb: int32 [4096], P('rank'), may hold values from 0 to 15
- compat: int32 [16, 16], replicated, may hold values from 0 to 1, as said below
- counts: int32 [384], P('dp'), may hold values from 32 to 256
Outputs:
- influence: float32 [384, 4096], P('dp', 'rank')
Inputs may be any that keep to these rules, and one draw needn't show every extreme that they name: compat has ones on its diagonal.
All inputs are finite; a program needn't handle non-finite values.
Results may differ from a plain program's by a relative error of at most 0.0003.
Values sent between devices are 32-bit elements; how exact they have to be, the bound alone decides.
No kernel may reach another device: no remote copies, remote signals or barrier semaphores. Data moves between devices by JAX's collectives and lax.ppermute only.
A program may use at most 128 MiB of HBM per device.

v0:
```python
import jax
import jax.numpy as jnp
from jax import lax
from jax.sharding import PartitionSpec as P


def outer_sum(table, factor, keep):
    grad_side = table[..., :factor] * keep[:, :, None]
    act_side = table[..., factor:]
    outer = jnp.einsum("sti,stj->sij", grad_side, act_side, precision=lax.Precision.HIGHEST)
    return outer.reshape(table.shape[0], factor * factor)


def per_device(acts, grads, proj_in, proj_out, queries, seg_emb, query_emb, compat, counts):
    segs, toks, _ = acts.shape
    factor = proj_in.shape[1]
    part_a = jnp.dot(
        acts.reshape(segs * toks, acts.shape[2]), proj_in, preferred_element_type=jnp.float32
    )
    part_g = jnp.dot(
        grads.reshape(segs * toks, grads.shape[2]), proj_out, preferred_element_type=jnp.float32
    )
    partial_proj = jnp.concatenate([part_g, part_a], axis=1).reshape(segs, toks, 2 * factor)
    whole = lax.psum(partial_proj, "rank")
    position = lax.iota(jnp.int32, toks)
    keep = (position[None, :] < counts[:, None]).astype(jnp.float32)
    feats = outer_sum(whole, factor, keep)
    raw = jnp.dot(feats, queries.T, precision=lax.Precision.HIGHEST)
    kinds = lax.iota(jnp.int32, compat.shape[0])
    onehot_seg = (seg_emb[:, None] == kinds[None, :]).astype(jnp.float32)
    onehot_query = (query_emb[:, None] == kinds[None, :]).astype(jnp.float32)
    table = jnp.dot(onehot_seg, compat.astype(jnp.float32), precision=lax.Precision.HIGHEST)
    allowed = jnp.dot(table, onehot_query.T, precision=lax.Precision.HIGHEST)
    raw = raw * allowed
    total = lax.psum(jnp.sum(raw * raw, axis=0), "dp")
    power = total / (segs * lax.axis_size("dp"))
    return raw / jnp.sqrt(power + 1e-06)[None, :]


def solution(mesh):
    return jax.shard_map(
        per_device,
        mesh=mesh,
        in_specs=(
            P("dp", None, "rank"),
            P("dp", None, "rank"),
            P("rank", None),
            P("rank", None),
            P("rank", None),
            P("dp"),
            P("rank"),
            P(),
            P("dp"),
        ),
        out_specs=P("dp", "rank"),
        check_vma=False,
    )
```

profile of v0, /device:TPU:0, one launch (start us, length us, event | category | flops | bytes accessed | tf_op | source)
XLA Modules:
  0.0 184.4 jit_solution(10990075989917965617)
XLA Ops:
  6.5 0.0 copy-start
  6.5 0.0 all-reduce.2.cloned.1.call-start
  6.5 8.6 %copy.14 = bf16[48,86,8,256]{3,2,0,1:T(8,128)(2,1)S(1)} copy(bf16[48,86,8,256]{3,2,1,0:T(8,128)(2,1)} %bitcast.17) | data formatting | bytes 33816576 | tf_op jit(solution)/shard_map/reshape | solution.py:21
  15.2 0.0 copy-done
  15.2 0.0 copy-start.2
  15.2 0.0 copy-start.3
  15.2 3.1 %fusion.10 = f32[12288,64]{0,1:T(8,128)S(1)} fusion(bf16[688,64]{0,1:T(8,128)(2,1)S(1)} %copy-done, bf16[12288,688]{0,1:T(8,128)(2,1)S(1)} %bitcast.14), kind=kOutput, calls=%fused_computation.20 | convolution fusion | flops 1082130432 | bytes 20142080 | tf_op jit(solution)/shard_map/dot_general | solution.py:20
  18.3 2.0 %fusion.8 = f32[12288,64]{0,1:T(8,128)S(1)} fusion(bf16[12288,256]{1,0:T(8,128)(2,1)S(1)} %bitcast.18, bf16[256,64]{0,1:T(8,128)(2,1)S(1)} %copy-done.3), kind=kOutput, calls=%fused_computation.18 | convolution fusion | flops 402653184 | bytes 9469952 | tf_op jit(solution)/shard_map/dot_general | solution.py:17
  20.3 0.6 pad_maximum_fusion
  20.9 3.6 %copy.16 = f32[16,48,8,256]{3,2,0,1:T(8,128)} copy(f32[16,48,8,256]{3,2,1,0:T(8,128)S(1)} %bitcast.16) | data formatting | bytes 12582912 | tf_op jit(solution)/shard_map/reshape | solution.py:23
  24.5 0.0 all-reduce.2.cloned.1.call-update
  24.5 0.7 copy-done.6
  25.2 0.2 fusion.5
  25.4 0.0 copy-done.5
  25.4 0.0 copy-start.1
  25.4 0.1 fusion.4
  25.5 123.8 %all-reduce.2.cloned.1.call-done = f32[48,256,128]{1,2,0:T(8,128)} async-done(((f32[48,256,128]{1,2,0:T(8,128)}), f32[48,256,128]{1,2,0:T(8,128)}) %all-reduce.2.cloned.1.call-update) | async-done | bytes 6291472 | tf_op jit(solution)/shard_map/psum | solution.py:24
  149.3 6.0 %fusion = f32[48,64,64]{2,1,0:T(8,128)S(1)} fusion(f32[48,256,128]{1,2,0:T(8,128)} %all-reduce.2.cloned.1.call-done, f32[48,256]{1,0:T(8,128)S(1)} %fusion.4), kind=kOutput, calls=%fused_computation.2 | convolution fusion | flops 604766208 | bytes 7127040 | tf_op jit(solution)/shard_map/sti,stj->sij/dot_general | solution.py:10
  155.2 0.5 reshape.40
  155.8 6.1 %fusion.9 = f32[48,256]{1,0:T(8,128)S(1)} fusion(f32[48,4096]{1,0:T(8,128)S(1)} %reshape.40, f32[256,4096]{1,0:T(8,128)} %param.13), kind=kOutput, calls=%fused_computation.19 | convolution fusion | flops 603979776 | bytes 5029888 | tf_op jit(solution)/shard_map/dot_general | solution.py:28
  161.8 0.3 multiply_reduce_fusion
  162.1 14.8 %psum.15 = f32[256]{0:T(256)S(1)} all-reduce(f32[256]{0:T(256)S(1)} %get-tuple-element.5), channel_id=1, replica_groups=mesh['dp'=8,'rank'=16] {'dp'}, use_global_device_ids=true, to_apply=%region_2.0 | all-reduce | flops 256 | bytes 2048 | tf_op jit(solution)/shard_map/psum | solution.py:35
  176.9 0.6 broadcast_divide_fusion
  177.6 0.0 copy-done.1
  (9 shorter events, 0.0 us)
Async XLA Ops:
  6.5 8.6 %copy-start = (bf16[688,64]{0,1:T(8,128)(2,1)S(1)}, bf16[688,64]{0,1:T(8,128)(2,1)}, u32[]{:S(2)}) copy-start(bf16[688,64]{0,1:T(8,128)(2,1)} %param.12) | copy-start | bytes 264196
  6.5 142.7 %all-reduce.2.cloned.1.call-start = ((), (), s32[]{:S(2)}) async-start(), calls=%async_computation | async-start | bytes 12582912 | tf_op jit(solution)/shard_map/psum | solution.py:24
  15.2 3.1 %copy-start.2 = (bf16[48,256,256]{2,1,0:T(8,128)(2,1)S(1)}, bf16[48,256,256]{2,1,0:T(8,128)(2,1)}, u32[]{:S(2)}) copy-start(bf16[48,256,256]{2,1,0:T(8,128)(2,1)} %param.9) | copy-start | bytes 18874372
  15.2 3.1 %copy-start.3 = (bf16[256,64]{0,1:T(8,128)(2,1)S(1)}, bf16[256,64]{0,1:T(8,128)(2,1)}, u32[]{:S(2)}) copy-start(bf16[256,64]{0,1:T(8,128)(2,1)} %param.11) | copy-start | bytes 98308
  24.5 0.7 copy-start.6
  24.5 0.7 copy-start.7
  24.5 0.9 copy-start.5
  25.4 152.2 %copy-start.1 = (bf16[688,64]{0,1:T(8,128)(2,1)S(1)}, bf16[688,64]{0,1:T(8,128)(2,1)}, u32[]{:S(2)}) copy-start(bf16[688,64]{0,1:T(8,128)(2,1)} %param.12) | copy-start | bytes 264196
  25.5 136.4 %copy-start.4 = (s32[256]{0:T(256)S(1)}, s32[256]{0:T(256)}, u32[]{:S(2)}) copy-start(s32[256]{0:T(256)} %param.15) | copy-start | bytes 3076
Sparse Core Ops, SparseCore 0:
  24.6 124.5 all-reduce.1
where the time goes:
time: 185 us; the launch traced here: 184 us
  waiting for transfers between devices  124 us (67%)
  matrix products  17.6 us (10%)
  blocking collectives  14.8 us (8%)
  between operations  13.5 us (7%)
  local copies, waits for them, and re-layouts  13.4 us (7%)
    psum x1, waiting for transfers between devices, per_device(): whole = lax.psum(partial_proj, 'rank')  124 us
    psum x1, blocking collectives, per_device(): total = lax.psum(jnp.sum(raw * raw, axis=0), 'dp')  14.8 us
    reshape x1, local copies, waits for them, and re-layouts, per_device(): grads.reshape(segs * toks, grads.shape[2])  8.61 us
    dot_general x1, matrix products, per_device(): raw = jnp.dot(feats, queries.T, precision=lax.Precision.HIGHEST)  6.07 us
    dot_general x1, matrix products, outer_sum(): jnp.einsum('sti,stj->sij', grad_side, act_side, precision=lax.Precision.H...  5.97 us
  transfers between devices with their start and end apart: 1, of which 1 were waited for; matrix products, arithmetic and copies ran while one was open for 0% of the time, Pallas kernels for 0%

commit v1 on v0

v1 whole, which is shorter than its diff:
```python
import functools

import jax
import jax.numpy as jnp
import numpy as np
from jax import lax
from jax.experimental import pallas as pl
from jax.experimental.pallas import tpu as pltpu
from jax.sharding import PartitionSpec as P

SIDE = 4
RANKS = SIDE * SIDE
SLOTS = 3
BF16 = jnp.bfloat16
F32 = jnp.float32
LADDER = (768,)


def at(x, y):
    return (x % SIDE) * SIDE + y % SIDE


def receiver(role, d, rank):
    x, y = divmod(rank, SIDE)
    even = (x + y + d) % 2 == 0
    return at(x + d, y) if even == (role == 1) else at(x, y + d)


def second(kind, rank):
    x, y = divmod(rank, SIDE)
    even = (x + y) % 2 == 0
    if kind == 3:
        return at(x, y + 2) if even else at(x + 2, y)
    step = 1 if kind == 1 else -1
    return at(x + step, y) if even else at(x, y + step)


def destinations(rank):
    order = []
    for d in range(SIDE):
        r1, r2 = receiver(1, d, rank), receiver(2, d, rank)
        order += [r1, second(3, r1), second(1, r2), second(2, r2)]
    return order


def slot_positions(rank):
    zig = 7 - rank // 2 if rank % 2 == 0 else 15 - rank // 2
    sums = [r + (7 - r // 2 if r % 2 == 0 else 15 - r // 2) for r in range(RANKS)]
    above = sum(s > sums[rank] or (s == sums[rank] and r > rank) for r, s in enumerate(sums))
    return [rank, RANKS + zig, 2 * RANKS + above]


def gathered(rank):
    x, y = divmod(rank, SIDE)
    return [at(x - dx, y - dy) for dy in range(SIDE) for dx in range(SIDE)]


PROJECT_POS = np.array([sum((slot_positions(q) for q in destinations(r)), []) for r in range(RANKS)], np.int32)
GATHER_POS = np.array([sum((slot_positions(q) for q in gathered(r)), []) for r in range(RANKS)], np.int32)
OWNER_POS = np.array([slot_positions(q) for q in range(RANKS)], np.int32).T.reshape(-1)
FIRST = {(role, d): [(r, receiver(role, d, r)) for r in range(RANKS)] for role in (1, 2) for d in range(1, SIDE)}
SECOND = {kind: [(r, second(kind, r)) for r in range(RANKS)] for kind in (1, 2, 3)}


def shift(dx, dy):
    return [(r, at(r // SIDE + dx, r % SIDE + dy)) for r in range(RANKS)]


def up(n, m):
    return (n + (m - 1)) // m * m


def project_kernel(part, cap, segs, cnts, *refs):
    acts, grads = refs[0:3], refs[3:6]
    w_in, w_out, out1, out2, spill = refs[6:]
    step = pl.program_id(0)
    toks = acts[0].shape[1]
    w_a = jnp.concatenate([jnp.zeros_like(w_in[...]), w_in[...]], axis=0)
    nt = (((1,), (1,)), ((), ()))

    def rows(k):
        side_a = lax.dot_general(acts[k][0], w_a, nt, preferred_element_type=F32)
        side_g = jnp.dot(w_out[...], grads[k][0], preferred_element_type=F32)
        return side_a + jnp.concatenate([side_g, jnp.zeros_like(side_g)], axis=0).T

    base = part * 12 + step * SLOTS
    off1 = pl.multiple_of(up(cnts[base], 8), 8)
    off2 = pl.multiple_of(off1 + up(cnts[base + 1], 8), 8)
    pieces = up(cnts[base + 2], 16) // 16

    def write(out):
        out[pl.ds(0, toks), :] = rows(0)
        out[pl.ds(off1, toks), :] = rows(1)
        spill[...] = rows(2)

        def piece(i, _):
            to = pl.multiple_of(off2 + i * 16, 8)
            out[pl.ds(to, 16), :] = spill[pl.ds(pl.multiple_of(i * 16, 16), 16), :]
            return 0

        lax.fori_loop(0, pieces, piece, 0)

    pl.when(step < 2)(lambda: write(out1))
    pl.when(step >= 2)(lambda: write(out2))


def project(part, cap, segs, cnts, acts, grads_t, w_in, w_out):
    toks, fa = acts.shape[1:]
    fg = grads_t.shape[1]

    def seg(k):
        return lambda i, s, c: (s[part * 12 + i * SLOTS + k], 0, 0)

    whole = lambda i, s, c: (0, 0)
    out = jax.ShapeDtypeStruct((2 * cap, 128), F32)
    return pl.pallas_call(
        functools.partial(project_kernel, part, cap),
        grid_spec=pltpu.PrefetchScalarGridSpec(
            num_scalar_prefetch=2,
            grid=(4,),
            in_specs=[pl.BlockSpec((1, toks, fa), seg(k)) for k in range(SLOTS)]
            + [pl.BlockSpec((1, fg, toks), seg(k)) for k in range(SLOTS)]
            + [pl.BlockSpec(w_in.shape, whole), pl.BlockSpec(w_out.shape, whole)],
            out_specs=[
                pl.BlockSpec((cap, 128), lambda i, s, c: (jnp.minimum(i, 1), 0)),
                pl.BlockSpec((cap, 128), lambda i, s, c: (jnp.maximum(i - 2, 0), 0)),
            ],
            scratch_shapes=[pltpu.VMEM((toks, 128), F32)],
        ),
        out_shape=(out, out),
        compiler_params=pltpu.CompilerParams(vmem_limit_bytes=24 * 2**20),
        cost_estimate=pl.CostEstimate(
            flops=12 * toks * 2 * 64 * (fa + fg),
            bytes_accessed=12 * toks * 2 * (fa + fg) + 4 * cap * 512,
            transcendentals=0,
        ),
        name="project",
    )(segs, cnts, acts, acts, acts, grads_t, grads_t, grads_t, w_in, w_out)


def split(x):
    hi = x.astype(BF16)
    return hi, (x - hi.astype(F32)).astype(BF16)


def outer_kernel(cnts, own, r1, r2, r3, out, pair):
    total = (own[...] + r1[...]) + (r2[...] + r3[...])
    cap = total.shape[0]
    row = lax.broadcasted_iota(jnp.int32, (cap, 128), 0)
    off1 = up(cnts[0], 8)
    off2 = off1 + up(cnts[1], 8)
    live = [
        row < cnts[0],
        (row >= off1) & (row < off1 + cnts[1]),
        (row >= off2) & (row < off2 + cnts[2]),
    ]
    total = jnp.where(live[0] | live[1] | live[2], total, 0.0)
    lane = lax.broadcasted_iota(jnp.int32, (cap, 128), 1)
    act = jnp.where(lane < 64, pltpu.roll(total, 64, 1), total)
    a_hi, a_lo = split(act)
    total_t = total.T[:64]
    col = lax.broadcasted_iota(jnp.int32, (64, cap), 1)
    live_t = [
        col < cnts[0],
        (col >= off1) & (col < off1 + cnts[1]),
        (col >= off2) & (col < off2 + cnts[2]),
    ]
    grad = jnp.concatenate([jnp.where(m, total_t, 0.0) for m in live_t], axis=0)
    g_hi, g_lo = split(grad)
    dot = functools.partial(jnp.dot, preferred_element_type=F32)
    pair[...] = dot(g_hi, a_hi) + (dot(g_hi, a_lo) + dot(g_lo, a_hi))
    first = pair[pl.ds(0, 96, stride=2), :]
    other = pair[pl.ds(1, 96, stride=2), :]
    lane = lax.broadcasted_iota(jnp.int32, (96, 128), 1)
    out[...] = jnp.where(lane < 64, first, other)


def outer(cnts, parts):
    cap = parts[0].shape[0]
    spec = pl.BlockSpec(memory_space=pltpu.VMEM)
    return pl.pallas_call(
        outer_kernel,
        in_specs=[pl.BlockSpec(memory_space=pltpu.SMEM)] + [spec] * 4,
        out_specs=spec,
        out_shape=jax.ShapeDtypeStruct((SLOTS * 32, 128), F32),
        scratch_shapes=[pltpu.VMEM((SLOTS * 64, 128), F32)],
        compiler_params=pltpu.CompilerParams(vmem_limit_bytes=24 * 2**20),
        cost_estimate=pl.CostEstimate(flops=6 * 192 * cap * 128, bytes_accessed=4 * cap * 512, transcendentals=0),
        name="outer",
    )(cnts, *parts)


def hop(x, pairs):
    return lax.ppermute(x, "rank", pairs)


def features(cap, segs, cnts, acts, grads_t, w_in, w_out):
    made = {}
    got = {}
    for d in (1, 3, 2, 0):
        made[1, d], made[2, d] = project(d, cap, segs, cnts, acts, grads_t, w_in, w_out)
        for role in (1, 2):
            got[role, d] = hop(made[role, d], FIRST[role, d]) if d else made[role, d]
    s1 = (got[1, 0] + got[1, 1]) + (got[1, 3] + got[1, 2])
    s2 = (got[2, 0] + got[2, 1]) + (got[2, 3] + got[2, 2])
    parts = [
        s1[:cap],
        hop(s2[:cap], SECOND[1]),
        hop(s2[cap:], SECOND[2]),
        hop(s1[cap:], SECOND[3]),
    ]
    return outer(cnts[:SLOTS], parts)


def score_kernel(segs, *refs):
    feats, (queries, seg_kind, query_kind, compat, raw_out, sums_out, placed) = refs[:4], refs[4:]
    step = pl.program_id(0)
    n = placed.shape[0]
    nt = (((1,), (1,)), ((), ()))

    @pl.when(step == 0)
    def _():
        placed[...] = jnp.zeros_like(placed)

    dot = functools.partial(lax.dot_general, dimension_numbers=nt, preferred_element_type=F32)
    total = placed[...]
    width = queries.shape[1] // 128
    for m in range(width):
        left = jnp.concatenate(
            [f[pl.ds(step * width + m, f.shape[0] // 32, stride=32), :] for f in feats], axis=0
        )
        l_hi, l_lo = split(left)
        q_hi, q_lo = split(queries[:, m * 128 : (m + 1) * 128])
        both = dot(jnp.concatenate([l_hi, l_lo], axis=0), q_hi)
        total = total + (both[:n] + both[n:]) + dot(l_hi, q_lo)
    placed[...] = total

    @pl.when(step == pl.num_programs(0) - 1)
    def _():
        for slot in range(n):
            raw_out[pl.ds(segs[slot], 1), :] = placed[slot : slot + 1, :]
        kinds = compat.shape[0]
        one_seg = (seg_kind[...] == lax.broadcasted_iota(jnp.int32, (n, kinds), 1)).astype(F32)
        nq = query_kind.shape[1]
        one_query = (query_kind[...] == lax.broadcasted_iota(jnp.int32, (kinds, nq), 0)).astype(F32)
        table = jnp.dot(one_seg, compat[...].astype(F32), preferred_element_type=F32)
        allowed = jnp.dot(table, one_query, preferred_element_type=F32)
        raw = raw_out[...] * allowed
        raw_out[...] = raw
        sums_out[...] = jnp.broadcast_to(jnp.sum(raw * raw, axis=0, keepdims=True), sums_out.shape)


def score(segs, feats, queries, seg_emb, query_emb, compat):
    n, nq = segs.shape[0], queries.shape[0]
    steps = 4
    fixed = lambda i, s: (0, 0)
    return pl.pallas_call(
        score_kernel,
        grid_spec=pltpu.PrefetchScalarGridSpec(
            num_scalar_prefetch=1,
            grid=(steps,),
            in_specs=[pl.BlockSpec(f.shape, fixed) for f in feats]
            + [
                pl.BlockSpec((nq, queries.shape[1] // steps), lambda i, s: (0, i)),
                pl.BlockSpec((n, 1), fixed),
                pl.BlockSpec((1, nq), fixed),
                pl.BlockSpec(compat.shape, fixed),
            ],
            out_specs=[pl.BlockSpec((n, nq), fixed), pl.BlockSpec((8, nq), fixed)],
            scratch_shapes=[pltpu.VMEM((n, nq), F32)],
        ),
        out_shape=(jax.ShapeDtypeStruct((n, nq), F32), jax.ShapeDtypeStruct((8, nq), F32)),
        compiler_params=pltpu.CompilerParams(vmem_limit_bytes=24 * 2**20),
        cost_estimate=pl.CostEstimate(flops=6 * n * nq * 4096, bytes_accessed=nq * 4096 * 4, transcendentals=0),
        name="score",
    )(segs, *feats, queries, seg_emb[:, None], query_emb[None, :], compat)


def per_device(acts, grads, proj_in, proj_out, queries, seg_emb, query_emb, compat, counts):
    segs_here = acts.shape[0]
    me = lax.axis_index("rank")
    grads_t = jnp.swapaxes(grads, 1, 2)
    w_in, w_out = proj_in.T, proj_out.T

    ids = lax.iota(jnp.int32, segs_here)
    before = (counts[None, :] > counts[:, None]) | (
        (counts[None, :] == counts[:, None]) & (ids[None, :] < ids[:, None])
    )
    place = jnp.sum(before.astype(jnp.int32), axis=1)

    def pick(positions, values):
        return jnp.sum(jnp.where(positions[:, None] == place[None, :], values[None, :], 0), axis=1)

    mine = jnp.asarray(PROJECT_POS)[me]
    segs, cnts = pick(mine, ids), pick(mine, counts)
    segs_gathered = pick(jnp.asarray(GATHER_POS)[me], ids)

    owned = features(LADDER[-1], segs, cnts, acts, grads_t, w_in, w_out)
    line = jnp.concatenate([owned] + [hop(owned, shift(d, 0)) for d in (1, 2, 3)], axis=0)
    feats = [line] + [hop(line, shift(0, d)) for d in (1, 2, 3)]
    raw, sums = score(segs_gathered, feats, queries, seg_emb, query_emb, compat)

    cores = 2
    groups = lax.axis_size("dp")
    total = sums + lax.ppermute(sums, "dp", [(i, i ^ 1) for i in range(groups)])
    around = [
        lax.ppermute(total, "dp", [(i, (i + cores * d) % groups) for i in range(groups)])
        for d in range(1, groups // cores)
    ]
    for other in around:
        total = total + other
    power = total[:1] / (segs_here * groups)
    return raw / jnp.sqrt(power + 1e-06)


def solution(mesh):
    return jax.shard_map(
        per_device,
        mesh=mesh,
        in_specs=(
            P("dp", None, "rank"),
            P("dp", None, "rank"),
            P("rank", None),
            P("rank", None),
            P("rank", None),
            P("dp"),
            P("rank"),
            P(),
            P("dp"),
        ),
        out_specs=P("dp", "rank"),
        check_vma=False,
    )
```

time: 185 us -> 129 us (0.70)
  waiting for transfers between devices: 124 us -> 61.3 us
  starting transfers between devices: 0.01 us -> 35.2 us
  matrix products: 17.6 us -> 0 us
  Pallas kernels: 0 us -> 16.1 us
  blocking collectives: 14.8 us -> 0 us
  between operations: 13.5 us -> 0.12 us
    psum x1 -> x0, waiting for transfers between devices: 124 us -> none  [per_device(): whole = lax.psum(partial_proj, 'rank')]
    ppermute x0 -> x19, waiting for transfers between devices: none -> 61.3 us  [the longest x15 57.5 us: hop(): return lax.ppermute(x, 'rank', pairs)]
    ppermute x0 -> x19, starting transfers between devices: none -> 35.2 us  [the longest x15 28.6 us: hop(): return lax.ppermute(x, 'rank', pairs)]
    dot_general x6 -> x0, matrix products: 17.6 us -> none  [the longest x1 6.07 us: per_device(): raw = jnp.dot(feats, queries.T, precision=lax.Precision.HIGHEST)]
    pallas_call x0 -> x6, Pallas kernels: none -> 16.1 us  [the longest x4 11.7 us: project(): pl.pallas_call(functools.partial(project_kernel, part, cap), grid_spec=pl...]
    psum x1 -> x0, blocking collectives: 14.8 us -> none  [per_device(): total = lax.psum(jnp.sum(raw * raw, axis=0), 'dp')]
    reshape x3 -> x0, local copies, waits for them, and re-layouts: 12.7 us -> none  [the longest x1 8.61 us: per_device(): grads.reshape(segs * toks, grads.shape[2])]
    unnamed x16, local copies, waits for them, and re-layouts: 0.7 us -> 12.4 us
  transfers between devices with their start and end apart: 1 -> 19, of which waited for: 1 -> 13; matrix products, arithmetic and copies ran while one was open for 0% -> 0% of each run, Pallas kernels for 0% -> 7%
where the time goes in v1:
time: 129 us
  waiting for transfers between devices  61.3 us (48%)
  starting transfers between devices  35.2 us (27%)
  Pallas kernels  16.1 us (12%)
  local copies, waits for them, and re-layouts  13.4 us (10%)
  other arithmetic  2.81 us (2%)
    ppermute x15, waiting for transfers between devices, hop(): return lax.ppermute(x, 'rank', pairs)  57.5 us
    ppermute x15, starting transfers between devices, hop(): return lax.ppermute(x, 'rank', pairs)  28.6 us
    unnamed x16, local copies, waits for them, and re-layouts  12.4 us
    pallas_call x4, Pallas kernels, project(): pl.pallas_call(functools.partial(project_kernel, part, cap), grid_spec=pl...  11.7 us
    ppermute x3, starting transfers between devices, per_device(): lax.ppermute(total, 'dp', [(i, (i + cores * d) % groups) for i in range(g...  6.48 us
    pallas_call x1, Pallas kernels, score(): pl.pallas_call(score_kernel, grid_spec=pltpu.PrefetchScalarGridSpec(num_s...  3.17 us
    ppermute x3, waiting for transfers between devices, per_device(): lax.ppermute(total, 'dp', [(i, (i + cores * d) % groups) for i in range(g...  2.59 us
  transfers between devices with their start and end apart: 19, of which 13 were waited for; matrix products, arithmetic and copies ran while one was open for 0% of the time, Pallas kernels for 7%

profile of v1, /device:TPU:0, one launch (start us, length us, event | category | flops | bytes accessed | tf_op | source)
XLA Modules:
  0.0 128.8 jit_solution(661896883376259079)
XLA Ops:
  2.5 5.8 %copy-done = bf16[48,256,688]{1,2,0:T(8,128)(2,1)S(1)} copy-done((bf16[48,256,688]{1,2,0:T(8,128)(2,1)S(1)}, bf16[48,256,688]{1,2,0:T(8,128)(2,1)}, u32[]{:S(2)}) %copy-start) | copy-done | bytes 16908312
  8.3 2.8 %copy-done.1 = bf16[48,256,256]{2,1,0:T(8,128)(2,1)S(1)} copy-done((bf16[48,256,256]{2,1,0:T(8,128)(2,1)S(1)}, bf16[48,256,256]{2,1,0:T(8,128)(2,1)}, u32[]{:S(2)}) %copy-start.1) | copy-done | bytes 6291480
  12.8 2.9 %project.5 = (f32[1536,128]{1,0:T(8,128)S(1)}, f32[1536,128]{1,0:T(8,128)S(1)}) custom-call(s32[48]{0:T(128)S(1)} %get-tuple-element.25.segs, s32[48]{0:T(128)S(1)} %get-tuple-element.26.cnts, bf16[48,256,256]{2,1,0:T(8,128)(2,1)S(1)} %copy-done.1, bf16[48,256,256]{2,1,0:T(8,128)(2,1)S(1)} %copy-done.1, bf16[48,256,256]{2,1,0:T(8,128)(2,1)S(1)} %copy-done.1, ...), custom_call_target="tpu_custom_call" | custom-call | flops 371195904 | bytes 7372800 | tf_op jit(solution)/shard_map/project/pallas_call | solution.py:116
  17.3 2.9 %project.7 = (f32[1536,128]{1,0:T(8,128)S(1)}, f32[1536,128]{1,0:T(8,128)S(1)}) custom-call(s32[48]{0:T(128)S(1)} %get-tuple-element.25.segs, s32[48]{0:T(128)S(1)} %get-tuple-element.26.cnts, bf16[48,256,256]{2,1,0:T(8,128)(2,1)S(1)} %copy-done.1, bf16[48,256,256]{2,1,0:T(8,128)(2,1)S(1)} %copy-done.1, bf16[48,256,256]{2,1,0:T(8,128)(2,1)S(1)} %copy-done.1, ...), custom_call_target="tpu_custom_call" | custom-call | flops 371195904 | bytes 7372800 | tf_op jit(solution)/shard_map/project/pallas_call | solution.py:116
  20.2 3.3 %collective-permute-start.5 = (f32[1536,128]{1,0:T(8,128)S(1)}, f32[1536,128]{1,0:T(8,128)S(1)}, u32[]{:S(2)}, u32[]{:S(2)}) collective-permute-start(f32[1536,128]{1,0:T(8,128)S(1)} %get-tuple-element.22), channel_id=1, source_target_pairs={{0,2},{1,9},{2,0},{3,11},{4,12},{5,7},{6,14},{7,5},{8,10},{9,1},{1... | collective-permute-start | bytes 2359304 | tf_op jit(solution)/shard_map/ppermute | solution.py:194
  23.5 3.0 %project.6 = (f32[1536,128]{1,0:T(8,128)S(1)}, f32[1536,128]{1,0:T(8,128)S(1)}) custom-call(s32[48]{0:T(128)S(1)} %get-tuple-element.25.segs, s32[48]{0:T(128)S(1)} %get-tuple-element.26.cnts, bf16[48,256,256]{2,1,0:T(8,128)(2,1)S(1)} %copy-done.1, bf16[48,256,256]{2,1,0:T(8,128)(2,1)S(1)} %copy-done.1, bf16[48,256,256]{2,1,0:T(8,128)(2,1)S(1)} %copy-done.1, ...), custom_call_target="tpu_custom_call" | custom-call | flops 371195904 | bytes 7372800 | tf_op jit(solution)/shard_map/project/pallas_call | solution.py:116
  28.6 2.7 %collective-permute-start.2 = (f32[1536,128]{1,0:T(8,128)S(1)}, f32[1536,128]{1,0:T(8,128)S(1)}, u32[]{:S(2)}, u32[]{:S(2)}) collective-permute-start(f32[1536,128]{1,0:T(8,128)S(1)} %get-tuple-element.18), channel_id=1, source_target_pairs={{0,8},{1,3},{2,10},{3,1},{4,6},{5,13},{6,4},{7,15},{8,0},{9,11},{1... | collective-permute-start | bytes 2359304 | tf_op jit(solution)/shard_map/ppermute | solution.py:194
  31.2 2.9 %project.4 = (f32[1536,128]{1,0:T(8,128)S(1)}, f32[1536,128]{1,0:T(8,128)S(1)}) custom-call(s32[48]{0:T(128)S(1)} %get-tuple-element.25.segs, s32[48]{0:T(128)S(1)} %get-tuple-element.26.cnts, bf16[48,256,256]{2,1,0:T(8,128)(2,1)S(1)} %copy-done.1, bf16[48,256,256]{2,1,0:T(8,128)(2,1)S(1)} %copy-done.1, bf16[48,256,256]{2,1,0:T(8,128)(2,1)S(1)} %copy-done.1, ...), custom_call_target="tpu_custom_call" | custom-call | flops 371195904 | bytes 7372800 | tf_op jit(solution)/shard_map/project/pallas_call | solution.py:116
  34.1 19.1 %collective-permute-done.3 = f32[1536,128]{1,0:T(8,128)S(1)} collective-permute-done((f32[1536,128]{1,0:T(8,128)S(1)}, f32[1536,128]{1,0:T(8,128)S(1)}, u32[]{:S(2)}, u32[]{:S(2)}) %collective-permute-start.3) | collective-permute-done | bytes 786464 | tf_op jit(solution)/shard_map/ppermute | solution.py:194
  53.2 3.0 %collective-permute-start.1 = (f32[1536,128]{1,0:T(8,128)S(1)}, f32[1536,128]{1,0:T(8,128)S(1)}, u32[]{:S(2)}, u32[]{:S(2)}) collective-permute-start(f32[1536,128]{1,0:T(8,128)S(1)} %get-tuple-element.17), channel_id=1, source_target_pairs={{0,3},{1,13},{2,1},{3,15},{4,0},{5,4},{6,2},{7,6},{8,11},{9,5},{10... | collective-permute-start | bytes 2359304 | tf_op jit(solution)/shard_map/ppermute | solution.py:194
  57.0 2.5 %collective-permute-start.6 = (f32[768,128]{1,0:T(8,128)S(1)}, f32[768,128]{1,0:T(8,128)S(1)}, u32[]{:S(2)}, u32[]{:S(2)}) collective-permute-start(f32[768,128]{1,0:T(8,128)S(1)} %get-tuple-element.31), channel_id=1, source_target_pairs={{0,4},{1,2},{2,6},{3,0},{4,5},{5,9},{6,7},{7,11},{8,12},{9,10},{10... | collective-permute-start | bytes 1179656 | tf_op jit(solution)/shard_map/ppermute | solution.py:194
  61.3 2.7 %collective-permute-done = f32[1536,128]{1,0:T(8,128)S(1)} collective-permute-done((f32[1536,128]{1,0:T(8,128)S(1)}, f32[1536,128]{1,0:T(8,128)S(1)}, u32[]{:S(2)}, u32[]{:S(2)}) %collective-permute-start) | collective-permute-done | bytes 786464 | tf_op jit(solution)/shard_map/ppermute | solution.py:194
  64.1 13.9 %collective-permute-done.1 = f32[1536,128]{1,0:T(8,128)S(1)} collective-permute-done((f32[1536,128]{1,0:T(8,128)S(1)}, f32[1536,128]{1,0:T(8,128)S(1)}, u32[]{:S(2)}, u32[]{:S(2)}) %collective-permute-start.1) | collective-permute-done | bytes 786464 | tf_op jit(solution)/shard_map/ppermute | solution.py:194
  79.6 11.2 %collective-permute-done.8.r3 = f32[768,128]{1,0:T(8,128)S(1)} collective-permute-done((f32[768,128]{1,0:T(8,128)S(1)}, f32[768,128]{1,0:T(8,128)S(1)}, u32[]{:S(2)}, u32[]{:S(2)}) %collective-permute-start.8) | collective-permute-done | bytes 393248 | tf_op jit(solution)/shard_map/ppermute | solution.py:194
  92.1 2.8 %collective-permute-start.10 = (f32[96,128]{1,0:T(8,128)S(1)}, f32[96,128]{1,0:T(8,128)S(1)}, u32[]{:S(2)}, u32[]{:S(2)}) collective-permute-start(f32[96,128]{1,0:T(8,128)S(1)} %outer.1), channel_id=1, source_target_pairs={{0,8},{1,9},{2,10},{3,11},{4,12},{5,13},{6,14},{7,15},{8,0},{9,1},... | collective-permute-start | bytes 147464 | tf_op jit(solution)/shard_map/ppermute | solution.py:194
  94.8 2.0 %collective-permute-start.9 = (f32[96,128]{1,0:T(8,128)S(1)}, f32[96,128]{1,0:T(8,128)S(1)}, u32[]{:S(2)}, u32[]{:S(2)}) collective-permute-start(f32[96,128]{1,0:T(8,128)S(1)} %outer.1), channel_id=1, source_target_pairs={{0,4},{1,5},{2,6},{3,7},{4,8},{5,9},{6,10},{7,11},{8,12},{9,13},{1... | collective-permute-start | bytes 147464 | tf_op jit(solution)/shard_map/ppermute | solution.py:194
  100.1 2.7 %collective-permute-start.12 = (f32[384,128]{1,0:T(8,128)S(1)}, f32[384,128]{1,0:T(8,128)S(1)}, u32[]{:S(2)}, u32[]{:S(2)}) collective-permute-start(f32[384,128]{1,0:T(8,128)S(1)} %pad_maximum_fusion.refs_0_), channel_id=1, source_target_pairs={{0,1},{1,2},{2,3},{3,0},{4,5},{5,6},{6,7},{7,4},{8,9},{9,10},{10,1... | collective-permute-start | bytes 589832 | tf_op jit(solution)/shard_map/ppermute | solution.py:194
  102.8 2.6 %collective-permute-start.13 = (f32[384,128]{1,0:T(8,128)S(1)}, f32[384,128]{1,0:T(8,128)S(1)}, u32[]{:S(2)}, u32[]{:S(2)}) collective-permute-start(f32[384,128]{1,0:T(8,128)S(1)} %pad_maximum_fusion.refs_0_), channel_id=1, source_target_pairs={{0,2},{1,3},{2,0},{3,1},{4,6},{5,7},{6,4},{7,5},{8,10},{9,11},{10,... | collective-permute-start | bytes 589832 | tf_op jit(solution)/shard_map/ppermute | solution.py:194
  105.7 4.0 %collective-permute-done.12.refs_1_ = f32[384,128]{1,0:T(8,128)S(1)} collective-permute-done((f32[384,128]{1,0:T(8,128)S(1)}, f32[384,128]{1,0:T(8,128)S(1)}, u32[]{:S(2)}, u32[]{:S(2)}) %collective-permute-start.12) | collective-permute-done | bytes 196640 | tf_op jit(solution)/shard_map/ppermute | solution.py:194
  109.7 2.8 %collective-permute-done.13.refs_2_ = f32[384,128]{1,0:T(8,128)S(1)} collective-permute-done((f32[384,128]{1,0:T(8,128)S(1)}, f32[384,128]{1,0:T(8,128)S(1)}, u32[]{:S(2)}, u32[]{:S(2)}) %collective-permute-start.13) | collective-permute-done | bytes 196640 | tf_op jit(solution)/shard_map/ppermute | solution.py:194
  112.5 2.2 %copy-done.2 = f32[256,4096]{1,0:T(8,128)S(1)} copy-done((f32[256,4096]{1,0:T(8,128)S(1)}, f32[256,4096]{1,0:T(8,128)}, u32[]{:S(2)}) %copy-start.2) | copy-done | bytes 4194328
  114.7 3.2 %score.1 = (f32[48,256]{1,0:T(8,128)S(1)}, f32[8,256]{1,0:T(8,128)S(1)}) custom-call(s32[48]{0:T(128)S(1)} %get-tuple-element.27.segs, f32[384,128]{1,0:T(8,128)S(1)} %pad_maximum_fusion.refs_0_, f32[384,128]{1,0:T(8,128)S(1)} %collective-permute-done.12.refs_1_, f32[384,128]{1,0:T(8,128)S(1)} %collective-permute-done.13.refs_2_, ...), custom_call_target="tpu_custom_call" | custom-call | flops 301989888 | bytes 4194304 | tf_op jit(solution)/shard_map/score/pallas_call | solution.py:257
  120.9 3.6 %collective-permute-start.17 = (f32[8,256]{1,0:T(8,128)S(1)}, f32[8,256]{1,0:T(8,128)S(1)}, u32[]{:S(2)}, u32[]{:S(2)}) collective-permute-start(f32[8,256]{1,0:T(8,128)S(1)} %add.47), channel_id=1, source_target_pairs={{0,64},{16,80},{32,96},{48,112},{64,0},{80,16},{96,32},{112,48},{1... | collective-permute-start | bytes 24584 | tf_op jit(solution)/shard_map/ppermute | solution.py:307
  126.3 1.9 %collective-permute-done.18 = f32[8,256]{1,0:T(8,128)S(1)} collective-permute-done((f32[8,256]{1,0:T(8,128)S(1)}, f32[8,256]{1,0:T(8,128)S(1)}, u32[]{:S(2)}, u32[]{:S(2)}) %collective-permute-start.18) | collective-permute-done | bytes 8224 | tf_op jit(solution)/shard_map/ppermute | solution.py:307
  (48 shorter events, 22.5 us)
Async XLA Ops:
  2.5 5.8 %copy-start = (bf16[48,256,688]{1,2,0:T(8,128)(2,1)S(1)}, bf16[48,256,688]{1,2,0:T(8,128)(2,1)}, u32[]{:S(2)}) copy-start(bf16[48,256,688]{1,2,0:T(8,128)(2,1)} %param.12) | copy-start | bytes 50724868
  8.3 2.8 %copy-start.1 = (bf16[48,256,256]{2,1,0:T(8,128)(2,1)S(1)}, bf16[48,256,256]{2,1,0:T(8,128)(2,1)}, u32[]{:S(2)}) copy-start(bf16[48,256,256]{2,1,0:T(8,128)(2,1)} %refs_2_.7) | copy-start | bytes 18874372
  15.7 37.6 %collective-permute-start.3 = (f32[1536,128]{1,0:T(8,128)S(1)}, f32[1536,128]{1,0:T(8,128)S(1)}, u32[]{:S(2)}, u32[]{:S(2)}) collective-permute-start(f32[1536,128]{1,0:T(8,128)S(1)} %get-tuple-element.20), channel_id=1, source_target_pairs={{0,4},{1,2},{2,6},{3,0},{4,5},{5,9},{6,7},{7,11},{8,12},{9,10},{10... | collective-permute-start | bytes 2359304 | tf_op jit(solution)/shard_map/ppermute | solution.py:194
  20.2 36.0 %collective-permute-start.5 = (f32[1536,128]{1,0:T(8,128)S(1)}, f32[1536,128]{1,0:T(8,128)S(1)}, u32[]{:S(2)}, u32[]{:S(2)}) collective-permute-start(f32[1536,128]{1,0:T(8,128)S(1)} %get-tuple-element.22), channel_id=1, source_target_pairs={{0,2},{1,9},{2,0},{3,11},{4,12},{5,7},{6,14},{7,5},{8,10},{9,1},{1... | collective-permute-start | bytes 2359304 | tf_op jit(solution)/shard_map/ppermute | solution.py:194
  26.5 30.3 %collective-permute-start.4 = (f32[1536,128]{1,0:T(8,128)S(1)}, f32[1536,128]{1,0:T(8,128)S(1)}, u32[]{:S(2)}, u32[]{:S(2)}) collective-permute-start(f32[1536,128]{1,0:T(8,128)S(1)} %get-tuple-element.21), channel_id=1, source_target_pairs={{0,12},{1,0},{2,14},{3,2},{4,7},{5,1},{6,5},{7,3},{8,4},{9,8},{10,... | collective-permute-start | bytes 2359304 | tf_op jit(solution)/shard_map/ppermute | solution.py:194
  27.6 36.5 %collective-permute-start = (f32[1536,128]{1,0:T(8,128)S(1)}, f32[1536,128]{1,0:T(8,128)S(1)}, u32[]{:S(2)}, u32[]{:S(2)}) collective-permute-start(f32[1536,128]{1,0:T(8,128)S(1)} %get-tuple-element.16), channel_id=1, source_target_pairs={{0,1},{1,5},{2,3},{3,7},{4,8},{5,6},{6,10},{7,4},{8,9},{9,13},{10,... | collective-permute-start | bytes 2359304 | tf_op jit(solution)/shard_map/ppermute | solution.py:194
  28.6 35.5 %collective-permute-start.2 = (f32[1536,128]{1,0:T(8,128)S(1)}, f32[1536,128]{1,0:T(8,128)S(1)}, u32[]{:S(2)}, u32[]{:S(2)}) collective-permute-start(f32[1536,128]{1,0:T(8,128)S(1)} %get-tuple-element.18), channel_id=1, source_target_pairs={{0,8},{1,3},{2,10},{3,1},{4,6},{5,13},{6,4},{7,15},{8,0},{9,11},{1... | collective-permute-start | bytes 2359304 | tf_op jit(solution)/shard_map/ppermute | solution.py:194
  53.2 24.7 %collective-permute-start.1 = (f32[1536,128]{1,0:T(8,128)S(1)}, f32[1536,128]{1,0:T(8,128)S(1)}, u32[]{:S(2)}, u32[]{:S(2)}) collective-permute-start(f32[1536,128]{1,0:T(8,128)S(1)} %get-tuple-element.17), channel_id=1, source_target_pairs={{0,3},{1,13},{2,1},{3,15},{4,0},{5,4},{6,2},{7,6},{8,11},{9,5},{10... | collective-permute-start | bytes 2359304 | tf_op jit(solution)/shard_map/ppermute | solution.py:194
  56.8 48.8 %copy-start.7 = (s32[48]{0:T(128)S(1)}, s32[48]{0:T(128)}, u32[]{:S(2)}) copy-start(s32[48]{0:T(128)} %param.16) | copy-start | bytes 580
  56.8 55.7 %copy-start.5 = (s32[16,16]{1,0:T(8,128)S(1)}, s32[16,16]{1,0:T(8,128)}, u32[]{:S(2)}) copy-start(s32[16,16]{1,0:T(8,128)} %refs_7_.1) | copy-start | bytes 3076
  56.8 55.7 %copy-start.6 = (s32[256]{0:T(256)S(1)}, s32[256]{0:T(256)}, u32[]{:S(2)}) copy-start(s32[256]{0:T(256)} %param.17) | copy-start | bytes 3076
  57.0 22.6 %collective-permute-start.6 = (f32[768,128]{1,0:T(8,128)S(1)}, f32[768,128]{1,0:T(8,128)S(1)}, u32[]{:S(2)}, u32[]{:S(2)}) collective-permute-start(f32[768,128]{1,0:T(8,128)S(1)} %get-tuple-element.31), channel_id=1, source_target_pairs={{0,4},{1,2},{2,6},{3,0},{4,5},{5,9},{6,7},{7,11},{8,12},{9,10},{10... | collective-permute-start | bytes 1179656 | tf_op jit(solution)/shard_map/ppermute | solution.py:194
  59.6 20.1 %collective-permute-start.7 = (f32[768,128]{1,0:T(8,128)S(1)}, f32[768,128]{1,0:T(8,128)S(1)}, u32[]{:S(2)}, u32[]{:S(2)}) collective-permute-start(f32[768,128]{1,0:T(8,128)S(1)} %get-tuple-element.30), channel_id=1, source_target_pairs={{0,12},{1,0},{2,14},{3,2},{4,7},{5,1},{6,5},{7,3},{8,4},{9,8},{10,... | collective-permute-start | bytes 1179656 | tf_op jit(solution)/shard_map/ppermute | solution.py:194
  78.2 12.6 %collective-permute-start.8 = (f32[768,128]{1,0:T(8,128)S(1)}, f32[768,128]{1,0:T(8,128)S(1)}, u32[]{:S(2)}, u32[]{:S(2)}) collective-permute-start(f32[768,128]{1,0:T(8,128)S(1)} %get-tuple-element.28), channel_id=1, source_target_pairs={{0,2},{1,9},{2,0},{3,11},{4,12},{5,7},{6,14},{7,5},{8,10},{9,1},{1... | collective-permute-start | bytes 1179656 | tf_op jit(solution)/shard_map/ppermute | solution.py:194
  92.1 6.0 %collective-permute-start.10 = (f32[96,128]{1,0:T(8,128)S(1)}, f32[96,128]{1,0:T(8,128)S(1)}, u32[]{:S(2)}, u32[]{:S(2)}) collective-permute-start(f32[96,128]{1,0:T(8,128)S(1)} %outer.1), channel_id=1, source_target_pairs={{0,8},{1,9},{2,10},{3,11},{4,12},{5,13},{6,14},{7,15},{8,0},{9,1},... | collective-permute-start | bytes 147464 | tf_op jit(solution)/shard_map/ppermute | solution.py:194
  94.8 4.1 %collective-permute-start.11 = (f32[96,128]{1,0:T(8,128)S(1)}, f32[96,128]{1,0:T(8,128)S(1)}, u32[]{:S(2)}, u32[]{:S(2)}) collective-permute-start(f32[96,128]{1,0:T(8,128)S(1)} %outer.1), channel_id=1, source_target_pairs={{0,12},{1,13},{2,14},{3,15},{4,0},{5,1},{6,2},{7,3},{8,4},{9,5},{1... | collective-permute-start | bytes 147464 | tf_op jit(solution)/shard_map/ppermute | solution.py:194
  94.8 5.3 %collective-permute-start.9 = (f32[96,128]{1,0:T(8,128)S(1)}, f32[96,128]{1,0:T(8,128)S(1)}, u32[]{:S(2)}, u32[]{:S(2)}) collective-permute-start(f32[96,128]{1,0:T(8,128)S(1)} %outer.1), channel_id=1, source_target_pairs={{0,4},{1,5},{2,6},{3,7},{4,8},{5,9},{6,10},{7,11},{8,12},{9,13},{1... | collective-permute-start | bytes 147464 | tf_op jit(solution)/shard_map/ppermute | solution.py:194
  100.1 9.5 %collective-permute-start.12 = (f32[384,128]{1,0:T(8,128)S(1)}, f32[384,128]{1,0:T(8,128)S(1)}, u32[]{:S(2)}, u32[]{:S(2)}) collective-permute-start(f32[384,128]{1,0:T(8,128)S(1)} %pad_maximum_fusion.refs_0_), channel_id=1, source_target_pairs={{0,1},{1,2},{2,3},{3,0},{4,5},{5,6},{6,7},{7,4},{8,9},{9,10},{10,1... | collective-permute-start | bytes 589832 | tf_op jit(solution)/shard_map/ppermute | solution.py:194
  102.8 9.7 %collective-permute-start.13 = (f32[384,128]{1,0:T(8,128)S(1)}, f32[384,128]{1,0:T(8,128)S(1)}, u32[]{:S(2)}, u32[]{:S(2)}) collective-permute-start(f32[384,128]{1,0:T(8,128)S(1)} %pad_maximum_fusion.refs_0_), channel_id=1, source_target_pairs={{0,2},{1,3},{2,0},{3,1},{4,6},{5,7},{6,4},{7,5},{8,10},{9,11},{10,... | collective-permute-start | bytes 589832 | tf_op jit(solution)/shard_map/ppermute | solution.py:194
  105.4 7.1 %collective-permute-start.14 = (f32[384,128]{1,0:T(8,128)S(1)}, f32[384,128]{1,0:T(8,128)S(1)}, u32[]{:S(2)}, u32[]{:S(2)}) collective-permute-start(f32[384,128]{1,0:T(8,128)S(1)} %pad_maximum_fusion.refs_0_), channel_id=1, source_target_pairs={{0,3},{1,0},{2,1},{3,2},{4,7},{5,4},{6,5},{7,6},{8,11},{9,8},{10,9... | collective-permute-start | bytes 589832 | tf_op jit(solution)/shard_map/ppermute | solution.py:194
  117.9 1.3 collective-permute-start.15
  119.1 6.5 %collective-permute-start.16 = (f32[8,256]{1,0:T(8,128)S(1)}, f32[8,256]{1,0:T(8,128)S(1)}, u32[]{:S(2)}, u32[]{:S(2)}) collective-permute-start(f32[8,256]{1,0:T(8,128)S(1)} %add.47), channel_id=1, source_target_pairs={{0,32},{16,48},{32,64},{48,80},{64,96},{80,112},{96,0},{112,16},{1... | collective-permute-start | bytes 24584 | tf_op jit(solution)/shard_map/ppermute | solution.py:307
  120.9 5.3 %collective-permute-start.17 = (f32[8,256]{1,0:T(8,128)S(1)}, f32[8,256]{1,0:T(8,128)S(1)}, u32[]{:S(2)}, u32[]{:S(2)}) collective-permute-start(f32[8,256]{1,0:T(8,128)S(1)} %add.47), channel_id=1, source_target_pairs={{0,64},{16,80},{32,96},{48,112},{64,0},{80,16},{96,32},{112,48},{1... | collective-permute-start | bytes 24584 | tf_op jit(solution)/shard_map/ppermute | solution.py:307
  124.5 3.7 %collective-permute-start.18 = (f32[8,256]{1,0:T(8,128)S(1)}, f32[8,256]{1,0:T(8,128)S(1)}, u32[]{:S(2)}, u32[]{:S(2)}) collective-permute-start(f32[8,256]{1,0:T(8,128)S(1)} %add.47), channel_id=1, source_target_pairs={{0,96},{16,112},{32,0},{48,16},{64,32},{80,48},{96,64},{112,80},{1... | collective-permute-start | bytes 24584 | tf_op jit(solution)/shard_map/ppermute | solution.py:307
  (3 other events, 3.8 us)
